TPU v7x, 128 devices: a whole 4x4x4 slice. The times are simulated.
128 devices in a mesh: replica: 8 (over x_hi, z), section: 16 (over y, x_lo, core).
Axes of the slice: x: 4 (x_hi: 2, x_lo: 2; x = x_hi * 2 + x_lo), y: 4, z: 4, core: 2. Of those that a mesh axis runs over, the one named last changes fastest.
Arguments:
- gradients: bfloat16 [8, 256, 512, 128], P('replica', 'section'), may hold values from -6 to 6
- master: float32 [256, 512, 128], P('section', 'replica'), may hold values from -0.25 to 0.25
- moment_one: float32 [256, 512, 128], P('section', 'replica'), may hold values from -4 to 4
- moment_two: float32 [256, 512, 128], P('section', 'replica'), may hold values from 0.01 to 4
- new_owner: int32 [256, 1], replicated, may hold values from 0 to 14; in each aligned block of 16 rows (0 to 15, 16 to 31, ...) at most 2 rows name the same one
Outputs:
- new_master: float32 [16, 16, 2, 512, 128], P('section', None, None, 'replica')
- new_moment_one: float32 [16, 16, 2, 512, 128], P('section', None, None, 'replica')
- new_moment_two: float32 [16, 16, 2, 512, 128], P('section', None, None, 'replica')
- new_weights: bfloat16 [16, 16, 2, 512, 128], P('section')
Inputs may be any that keep to these rules, and one draw needn't show every extreme that they name: `new_owner`: among the 16 blocks of one old section, no new section is named more than 2 times. No block goes to section 15.
All inputs are finite; a program needn't handle non-finite values.
Results may differ from a plain program's by a relative error of at most 0.01.
Values may be sent and summed in bfloat16 or wider, within the bound.
A program may use at most 64 MiB of HBM per device.

v0:
```python
import jax
import jax.numpy as jnp
from jax import lax
from jax.sharding import PartitionSpec as P

PAIR = 2


beta_one = 0.9
beta_two = 0.95
step_count = 10.0
learn_rate = 0.01
decay_rate = 0.1
epsilon = 1e-08
correct_one = 1.0 - beta_one**step_count
correct_two = 1.0 - beta_two**step_count


def adamw_update(master, moment_one, moment_two, gradient):
    upd_one = beta_one * moment_one + (1.0 - beta_one) * gradient
    upd_two = beta_two * moment_two + (1.0 - beta_two) * gradient * gradient
    direction = upd_one / correct_one / (jnp.sqrt(upd_two / correct_two) + epsilon)
    upd_master = master - learn_rate * (direction + decay_rate * master)
    return (upd_master, upd_one, upd_two)


def place_table(owners, source, sections, pair_cap, per_section):
    own_targets = lax.dynamic_slice_in_dim(owners, source * per_section, per_section)
    indices = jnp.arange(per_section, dtype=jnp.int32)
    matches = (own_targets[:, None] == own_targets[None, :]) & (indices[None, :] < indices[:, None])
    position = jnp.sum(matches.astype(jnp.int32), axis=1)
    section_ids = jnp.arange(sections, dtype=jnp.int32)[:, None, None]
    slot_ids = jnp.arange(pair_cap, dtype=jnp.int32)[None, :, None]
    selected = (own_targets[None, None, :] == section_ids) & (position[None, None, :] == slot_ids)
    chosen = jnp.sum(jnp.where(selected, indices[None, None, :], 0), axis=2).reshape(-1)
    filled = jnp.any(selected, axis=2).reshape(-1)
    return (chosen, filled)


def pack(values, chosen, filled, sections, pair_cap):
    gathered = jnp.take(values, chosen, axis=0)
    masked = jnp.where(filled[:, None, None], gathered, jnp.zeros((), values.dtype))
    return masked.reshape((sections, pair_cap) + values.shape[1:])


def body(gradients, master, moment_one, moment_two, new_owner):
    sections = lax.axis_size("section")
    source = lax.axis_index("section")
    per_section = master.shape[0]
    owners = new_owner[:, 0]
    chosen, filled = place_table(owners, source, sections, PAIR, per_section)
    packed_grads = pack(gradients[0], chosen, filled, sections, PAIR)
    arrived = lax.all_to_all(packed_grads, "section", split_axis=0, concat_axis=0, tiled=True)
    arrived_state = (
        lax.all_to_all(
            pack(master, chosen, filled, sections, PAIR),
            "section",
            split_axis=0,
            concat_axis=0,
            tiled=True,
        ),
        lax.all_to_all(
            pack(moment_one, chosen, filled, sections, PAIR),
            "section",
            split_axis=0,
            concat_axis=0,
            tiled=True,
        ),
        lax.all_to_all(
            pack(moment_two, chosen, filled, sections, PAIR),
            "section",
            split_axis=0,
            concat_axis=0,
            tiled=True,
        ),
    )
    summed = lax.psum_scatter(
        arrived.astype(jnp.float32).astype(jnp.bfloat16), "replica", scatter_dimension=2, tiled=True
    ).astype(jnp.float32)
    out_master, out_one, out_two = adamw_update(
        arrived_state[0], arrived_state[1], arrived_state[2], summed
    )
    weights = lax.all_gather(out_master.astype(jnp.bfloat16), "replica", axis=2, tiled=True)
    return (out_master[None], out_one[None], out_two[None], weights[None])


def solution(mesh):
    placed = (
        P("replica", "section", None, None),
        P("section", "replica", None),
        P("section", "replica", None),
        P("section", "replica", None),
        P(),
    )
    return jax.shard_map(
        body,
        mesh=mesh,
        in_specs=placed,
        out_specs=(
            P("section", None, None, "replica", None),
            P("section", None, None, "replica", None),
            P("section", None, None, "replica", None),
            P("section", None, None, None, None),
        ),
        check_vma=False,
    )
```

profile of v0, /device:TPU:1, one launch (start us, length us, event | category | flops | bytes accessed | tf_op | source)
XLA Modules:
  0.0 252.0 jit_solution(11651037939650974444)
XLA Ops:
  7.2 0.0 copy-start
  7.2 0.0 reduce-scatter.2.cloned.1.call-start
  7.2 0.9 dynamic-slice_bitcast_fusion
  8.1 0.2 convert_reduce_fusion
  8.3 0.1 and_reduce_fusion
  8.4 0.1 fusion.4
  8.6 0.1 copy.10
  8.6 0.1 copy.9
  8.7 0.1 copy.12
  8.8 0.1 reshape.124
  8.9 0.0 copy-done
  9.0 3.1 %gather_fusion = bf16[32,512,128]{2,1,0:T(8,128)(2,1)} fusion(bf16[16,512,128]{2,1,0:T(8,128)(2,1)S(1)} %bitcast.15, s32[1024]{0:T(1024)S(1)} %pad_clamp_fusion), kind=kCustom, calls=%fused_computation.3 | custom fusion | bytes 8388736 | tf_op jit(solution)/shard_map/jit(_take)/gather | solution.py:41
  12.1 2.7 %select_select_fusion = bf16[16,2,512,128]{3,2,1,0:T(8,128)(2,1)S(1)} fusion(bf16[16,2,512,128]{3,2,1,0:T(8,128)(2,1)} %bitcast.16, pred[16,2]{1,0:T(8,128)(4,1)S(1)} %copy.12, pred[16,2]{1,0:T(8,128)(4,1)S(1)} %copy.9), kind=kLoop, calls=%fused_computation.4 | loop fusion | flops 4194304 | bytes 8388672 | tf_op jit(solution)/shard_map/jit(_where)/select_n | solution.py:42
  14.8 55.9 %all_to_all.20 = bf16[16,2,512,128]{3,2,1,0:T(8,128)(2,1)} all-to-all(bf16[16,2,512,128]{3,2,1,0:T(8,128)(2,1)S(1)} %select_select_fusion), channel_id=1, replica_groups=mesh['replica'=8,'section'=16] {'section'}, dimensions={0} | all-to-all | bytes 8388608 | tf_op jit(solution)/shard_map/all_to_all | solution.py:53
  70.7 0.0 reduce-scatter.2.cloned.1.call-update
  70.7 0.0 all-gather.2.cloned.1.call-start
  70.8 0.1 broadcast_in_dim.86
  70.9 0.1 reshape.121
  71.0 1.7 gather_fusion.3
  72.7 2.6 %gather_fusion.2 = f32[32,64,128]{2,1,0:T(8,128)} fusion(f32[16,64,128]{2,1,0:T(8,128)} %param.9, s32[1024]{0:T(1024)S(1)} %pad_clamp_fusion.1), kind=kCustom, calls=%fused_computation.1.clone | custom fusion | bytes 2097280 | tf_op jit(solution)/shard_map/jit(_take)/gather | solution.py:41
  75.3 2.6 %gather_fusion.1 = f32[32,64,128]{2,1,0:T(8,128)} fusion(f32[16,64,128]{2,1,0:T(8,128)} %param.8, s32[1024]{0:T(1024)S(1)} %pad_clamp_fusion.1), kind=kCustom, calls=%fused_computation.clone | custom fusion | bytes 2097280 | tf_op jit(solution)/shard_map/jit(_take)/gather | solution.py:41
  77.9 2.1 select_select_fusion.2
  80.0 23.2 %all_to_all.21 = f32[16,2,64,128]{3,2,1,0:T(8,128)S(1)} all-to-all(f32[16,2,64,128]{3,2,1,0:T(8,128)S(1)} %bitcast.20), channel_id=1, replica_groups=mesh['replica'=8,'section'=16] {'section'}, dimensions={0} | all-to-all | bytes 2097152 | tf_op jit(solution)/shard_map/all_to_all | solution.py:69
  103.2 25.0 %all_to_all.22 = f32[16,2,64,128]{3,2,1,0:T(8,128)} all-to-all(f32[16,2,64,128]{3,2,1,0:T(8,128)S(1)} %bitcast.19), channel_id=1, replica_groups=mesh['replica'=8,'section'=16] {'section'}, dimensions={0} | all-to-all | bytes 2097152 | tf_op jit(solution)/shard_map/all_to_all | solution.py:62
  128.2 20.6 %all_to_all.23 = f32[16,2,64,128]{3,2,1,0:T(8,128)} all-to-all(f32[16,2,64,128]{3,2,1,0:T(8,128)S(1)} %bitcast.18), channel_id=1, replica_groups=mesh['replica'=8,'section'=16] {'section'}, dimensions={0} | all-to-all | bytes 2097152 | tf_op jit(solution)/shard_map/all_to_all | solution.py:55
  148.8 16.2 %reduce-scatter.2.cloned.1.call-done = bf16[16,2,64,128]{3,2,1,0:T(8,128)(2,1)} async-done(((bf16[16,2,512,128]{3,2,1,0:T(8,128)(2,1)}), bf16[16,2,64,128]{3,2,1,0:T(8,128)(2,1)}) %reduce-scatter.2.cloned.1.call-update) | async-done | bytes 524304 | tf_op jit(solution)/shard_map/reduce_scatter | solution.py:77
  165.0 4.4 %fusion.7 = (bf16[16,2,64,128]{3,2,1,0:T(8,128)(2,1)}, f32[16,2,64,128]{3,2,1,0:T(8,128)}, f32[1,16,2,64,128]{4,3,2,1,0:T(8,128)}, f32[1,16,2,64,128]{4,3,2,1,0:T(8,128)}) fusion(f32[16,2,64,128]{3,2,1,0:T(8,128)} %all_to_all.23, f32[16,2,64,128]{3,2,1,0:T(8,128)S(1)} %all_to_all.21, bf16[16,2,64,128]{3,2,1,0:T(8,128)(2,1)} %reduce-scatter.2.cloned.1.call-done, ...), kind=kLoop, calls=%fused_computation.32 | loop fusion | flops 4456448 | bytes 7340032 | tf_op jit(solution)/shard_map/convert_element_type | solution.py:83
  169.4 0.0 all-gather.2.cloned.1.call-update
  169.4 71.1 %all-gather.2.cloned.1.call-done = bf16[16,2,512,128]{3,2,1,0:T(8,128)(2,1)} async-done(((bf16[16,2,64,128]{3,2,1,0:T(8,128)(2,1)}), bf16[16,2,512,128]{3,2,1,0:T(8,128)(2,1)}) %all-gather.2.cloned.1.call-update) | async-done | bytes 4194320 | tf_op jit(solution)/shard_map/all_gather | solution.py:83
  240.5 4.7 %copy.15 = bf16[1,16,2,512,128]{4,3,2,1,0:T(8,128)(2,1)} copy(bf16[1,16,2,512,128]{4,3,2,1,0:T(8,128)(2,1)} %bitcast.17) | data formatting | bytes 8388608
  (8 shorter events, 0.1 us)
Async XLA Ops:
  7.2 1.8 copy-start
  7.2 157.8 %reduce-scatter.2.cloned.1.call-start = ((), (), s32[]{:S(2)}) async-start(), calls=%async_computation.5 | async-start | bytes 4718592 | tf_op jit(solution)/shard_map/reduce_scatter | solution.py:77
  70.7 169.8 %all-gather.2.cloned.1.call-start = ((), (), s32[]{:S(2)}) async-start(), calls=%async_computation.6 | async-start | bytes 4718592 | tf_op jit(solution)/shard_map/all_gather | solution.py:83
Sparse Core Ops, SparseCore 0:
  70.9 94.0 reduce-scatter.1
  169.5 70.9 all-gather.1
where the time goes:
time: 253 us; the launch traced here: 252 us
  blocking collectives  125 us (49%)
  waiting for transfers between devices  87.4 us (35%)
  local copies, waits for them, and re-layouts  16.1 us (6%)
  between operations  14.1 us (6%)
  other arithmetic  9.64 us (4%)
    all_gather x1, waiting for transfers between devices, body(): lax.all_gather(out_master.astype(jnp.bfloat16), 'replica', axis=2, tiled=...  71.1 us
    all_to_all x1, blocking collectives, body(): lax.all_to_all(packed_grads, 'section', split_axis=0, concat_axis=0, tile...  55.9 us
    all_to_all x1, blocking collectives, body(): lax.all_to_all(pack(moment_one, chosen, filled, sections, PAIR), 'section...  25 us
    all_to_all x1, blocking collectives, body(): lax.all_to_all(pack(moment_two, chosen, filled, sections, PAIR), 'section...  23.2 us
    all_to_all x1, blocking collectives, body(): lax.all_to_all(pack(master, chosen, filled, sections, PAIR), 'section', s...  20.6 us
    reduce_scatter x1, waiting for transfers between devices, body(): lax.psum_scatter(arrived.astype(jnp.float32).astype(jnp.bfloat16), 'repli...  16.2 us
    gather x4, local copies, waits for them, and re-layouts, pack(): gathered = jnp.take(values, chosen, axis=0)  10 us
  transfers between devices with their start and end apart: 2, of which 2 were waited for; matrix products, arithmetic and copies ran while one was open for 4% of the time, Pallas kernels for 0%

commit v1 on v0

v1 whole, which is shorter than its diff:
```python
import functools

import jax
import jax.numpy as jnp
from jax import lax
from jax.experimental import pallas as pl
from jax.experimental.pallas import tpu as pltpu
from jax.sharding import PartitionSpec as P

MESH = pl.DeviceIdType.MESH
PAIR = 2
PARTS = 2

beta_one = 0.9
beta_two = 0.95
step_count = 10.0
learn_rate = 0.01
decay_rate = 0.1
epsilon = 1e-08
correct_one = 1.0 - beta_one**step_count
correct_two = 1.0 - beta_two**step_count


def adamw_update(master, moment_one, moment_two, gradient):
    upd_one = beta_one * moment_one + (1.0 - beta_one) * gradient
    upd_two = beta_two * moment_two + (1.0 - beta_two) * gradient * gradient
    direction = upd_one / correct_one / (jnp.sqrt(upd_two / correct_two) + epsilon)
    upd_master = master - learn_rate * (direction + decay_rate * master)
    return (upd_master, upd_one, upd_two)


def kernel(
    sections,
    owner_ref,
    grads_ref,
    master_ref,
    one_ref,
    two_ref,
    out_master,
    out_one,
    out_two,
    weights,
    own,
    mid_own,
    mid_in,
    mid_out,
    near,
    half_out,
    half_in,
    upd,
    sendbuf,
    moments,
    chosen,
    filled,
    load_sem,
    step_send,
    step_recv,
    mid_send,
    mid_recv,
    half_send,
    half_recv,
    mom_send,
    mom_recv,
    own_send,
    own_recv,
    far_send,
    far_recv,
    ring_send,
    ring_recv,
    fwd_send,
    fwd_recv,
):
    blocks = master_ref.shape[0]
    rows = master_ref.shape[1]
    part_rows = rows // PARTS
    r = lax.axis_index("replica")
    s = lax.axis_index("section")
    xh = r // 4
    z = r % 4
    up = lax.rem(z + 1, 4)
    down = lax.rem(z + 3, 4)
    opposite = lax.rem(z + 2, 4)
    dev_up = (xh * 4 + up, s)
    dev_down = (xh * 4 + down, s)
    partner = (1 - xh) * 4 + z

    def part(c):
        return pl.ds(c * part_rows, part_rows)

    def remote(src, dst, send, recv, device):
        return pltpu.make_async_remote_copy(
            src_ref=src, dst_ref=dst, send_sem=send, recv_sem=recv,
            device_id=device, device_id_type=MESH,
        )

    loads = []
    for c in range(PARTS):
        for k, (src, dst) in enumerate((
            (grads_ref.at[:, 0, up, part(c)], mid_own.at[0, :, part(c)]),
            (grads_ref.at[:, 1, down, part(c)], mid_own.at[1, :, part(c)]),
            (grads_ref.at[:, :, z, part(c)], own.at[:, :, part(c)]),
        )):
            copy = pltpu.make_async_copy(src, dst, load_sem.at[c, k])
            copy.start()
            loads.append(copy)

    barrier = pltpu.get_barrier_semaphore()
    pl.semaphore_signal(barrier, inc=1, device_id=dev_up, device_id_type=MESH)
    pl.semaphore_signal(barrier, inc=1, device_id=dev_down, device_id_type=MESH)
    pl.semaphore_signal(barrier, inc=1, device_id=(partner, s), device_id_type=MESH)

    def greet(i, _):
        t = lax.rem(s + i, sections)
        pl.semaphore_signal(barrier, inc=1, device_id=(r, t), device_id_type=MESH)
        pl.semaphore_signal(barrier, inc=1, device_id=(partner, t), device_id_type=MESH)
        return 0

    lax.fori_loop(1, sections, greet, 0)
    pl.semaphore_wait(barrier, 3 + 2 * (sections - 1))

    first = []
    for c in range(PARTS):
        rc = part(c)
        first.append((
            remote(grads_ref.at[:, 0, opposite, rc], mid_in.at[0, :, rc], step_send.at[c, 0], step_recv.at[c, 0], dev_up),
            remote(grads_ref.at[:, 1, opposite, rc], mid_in.at[1, :, rc], step_send.at[c, 1], step_recv.at[c, 1], dev_down),
            remote(grads_ref.at[:, 1, up, rc], near.at[0, 1, :, rc], step_send.at[c, 2], step_recv.at[c, 2], dev_up),
            remote(grads_ref.at[:, 0, down, rc], near.at[1, 0, :, rc], step_send.at[c, 3], step_recv.at[c, 3], dev_down),
        ))
        for copy in first[c]:
            copy.start()

    for t in range(sections):
        one_at = jnp.int32(0)
        last_at = jnp.int32(0)
        count = jnp.int32(0)
        for i in reversed(range(blocks)):
            same = owner_ref[0, s * blocks + i] == t
            one_at = jnp.where(same, i, one_at)
            last_at = jnp.where(same & (count == 0), i, last_at)
            count = count + jnp.where(same, 1, 0)
        chosen[t * PAIR] = one_at
        chosen[t * PAIR + 1] = last_at
        filled[t * PAIR] = jnp.where(count > 0, 1, 0)
        filled[t * PAIR + 1] = jnp.where(count > 1, 1, 0)

    second = [None] * PARTS

    def join(c):
        rc = part(c)
        second[c] = (
            remote(mid_out.at[0, :, rc], near.at[0, 0, :, rc], mid_send.at[c, 0], mid_recv.at[c, 0], dev_up),
            remote(mid_out.at[1, :, rc], near.at[1, 1, :, rc], mid_send.at[c, 1], mid_recv.at[c, 1], dev_down),
        )
        for h in range(2):
            loads[3 * c + h].wait()
            first[c][h].wait_recv()

            def add(b, _, h=h):
                mid_out[h, b, rc] = (
                    mid_in[h, b, rc].astype(jnp.float32) + mid_own[h, b, rc].astype(jnp.float32)
                ).astype(jnp.bfloat16)
                return 0

            lax.fori_loop(0, blocks, add, 0)
            second[c][h].start()

    def z_sum(c, b, h):
        rc = part(c)
        return (
            own[b, h, rc].astype(jnp.float32)
            + near[0, h, b, rc].astype(jnp.float32)
            + near[1, h, b, rc].astype(jnp.float32)
        )

    third = [None] * PARTS

    def cross(c):
        rc = part(c)
        loads[3 * c + 2].wait()
        first[c][2].wait_recv()
        first[c][3].wait_recv()
        second[c][0].wait_recv()
        second[c][1].wait_recv()

        def add(b, _):
            half_out[b, rc] = z_sum(c, b, 1 - xh).astype(jnp.bfloat16)
            return 0

        lax.fori_loop(0, blocks, add, 0)
        third[c] = remote(half_out.at[:, rc], half_in.at[:, rc], half_send.at[c], half_recv.at[c], (partner, s))
        third[c].start()

    def mom_copy(c, t):
        return remote(
            sendbuf.at[t, pl.ds(1, 2), :, part(c)], moments.at[s, :, :, part(c)],
            mom_send.at[c, t], mom_recv.at[c, s], (r, t),
        )

    def own_copy(c, t):
        return remote(
            sendbuf.at[t, 0, :, part(c)], weights.at[s, :, xh, z, part(c)],
            own_send.at[c, t], own_recv.at[c, s], (r, t),
        )

    def far_copy(c, t):
        return remote(
            sendbuf.at[t, 0, :, part(c)], weights.at[s, :, xh, z, part(c)],
            far_send.at[c, t], far_recv.at[c, s], (partner, t),
        )

    def update(c):
        rc = part(c)
        third[c].wait_recv()

        def step(b, _):
            gradient = z_sum(c, b, xh) + half_in[b, rc].astype(jnp.float32)
            new = adamw_update(master_ref[b, rc], one_ref[b, rc], two_ref[b, rc], gradient)
            for k in range(3):
                upd[k, b, rc] = new[k].astype(jnp.bfloat16)
            return 0

        lax.fori_loop(0, blocks, step, 0)

        def pack(t):
            for j in range(PAIR):
                index = chosen[t * PAIR + j]
                there = filled[t * PAIR + j] != 0
                for k in range(3):
                    value = upd[k, index, rc]
                    sendbuf[t, k, j, rc] = jnp.where(there, value, jnp.zeros_like(value))

        def deliver(i, _):
            t = lax.rem(s + i, sections)
            pack(t)
            own_copy(c, t).start()
            far_copy(c, t).start()
            mom_copy(c, t).start()
            return 0

        lax.fori_loop(1, sections, deliver, 0)
        pack(s)
        far_copy(c, s).start()
        for j in range(PAIR):
            weights[s, j, xh, z, rc] = sendbuf[s, 0, j, rc]
            moments[s, 0, j, rc] = sendbuf[s, 1, j, rc]
            moments[s, 1, j, rc] = sendbuf[s, 2, j, rc]

    def arrived(ref_of, sem_of, device):
        return remote(ref_of, ref_of, sem_of, sem_of, device)

    ring = [None] * PARTS

    def gather(c):
        rc = part(c)

        def take(i, _):
            t = lax.rem(s + i, sections)
            arrived(weights.at[t, :, xh, z, rc], own_recv.at[c, t], (r, t)).wait_recv()
            arrived(weights.at[t, :, 1 - xh, z, rc], far_recv.at[c, t], (partner, t)).wait_recv()
            return 0

        lax.fori_loop(1, sections, take, 0)
        arrived(weights.at[s, :, 1 - xh, z, rc], far_recv.at[c, s], (partner, s)).wait_recv()
        ring[c] = (
            remote(weights.at[:, :, 0, z, rc], weights.at[:, :, 0, z, rc], ring_send.at[c, 0], ring_recv.at[c, 0], dev_up),
            remote(weights.at[:, :, 1, z, rc], weights.at[:, :, 1, z, rc], ring_send.at[c, 1], ring_recv.at[c, 1], dev_down),
            remote(weights.at[:, :, 1, z, rc], weights.at[:, :, 1, z, rc], ring_send.at[c, 2], ring_recv.at[c, 2], dev_up),
            remote(weights.at[:, :, 0, z, rc], weights.at[:, :, 0, z, rc], ring_send.at[c, 3], ring_recv.at[c, 3], dev_down),
        )
        for copy in ring[c]:
            copy.start()

    onward = [None] * PARTS

    def forward(c):
        rc = part(c)
        onward[c] = (
            remote(weights.at[:, :, 0, down, rc], weights.at[:, :, 0, down, rc], fwd_send.at[c, 0], fwd_recv.at[c, 0], dev_up),
            remote(weights.at[:, :, 1, up, rc], weights.at[:, :, 1, up, rc], fwd_send.at[c, 1], fwd_recv.at[c, 1], dev_down),
        )
        arrived(weights.at[:, :, 0, down, rc], ring_recv.at[c, 0], dev_down).wait_recv()
        onward[c][0].start()
        arrived(weights.at[:, :, 1, up, rc], ring_recv.at[c, 1], dev_up).wait_recv()
        onward[c][1].start()

    def state(c):
        rc = part(c)

        def take(i, _):
            t = lax.rem(s + i, sections)
            arrived(moments.at[t, :, :, rc], mom_recv.at[c, t], (r, t)).wait_recv()
            return 0

        lax.fori_loop(1, sections, take, 0)

        def widen(t, _):
            for j in range(PAIR):
                out_master[t, j, rc] = weights[t, j, xh, z, rc].astype(jnp.float32)
                out_one[t, j, rc] = moments[t, 0, j, rc].astype(jnp.float32)
                out_two[t, j, rc] = moments[t, 1, j, rc].astype(jnp.float32)
            return 0

        lax.fori_loop(0, sections, widen, 0)

    stages = (join, cross, update, gather, forward, state)
    for tick in range(PARTS + len(stages) - 1):
        for number in reversed(range(len(stages))):
            c = tick - number
            if 0 <= c < PARTS:
                stages[number](c)

    for c in range(PARTS):
        rc = part(c)
        arrived(weights.at[:, :, 1, down, rc], ring_recv.at[c, 2], dev_down).wait_recv()
        arrived(weights.at[:, :, 0, up, rc], ring_recv.at[c, 3], dev_up).wait_recv()
        arrived(weights.at[:, :, 0, opposite, rc], fwd_recv.at[c, 0], dev_down).wait_recv()
        arrived(weights.at[:, :, 1, opposite, rc], fwd_recv.at[c, 1], dev_up).wait_recv()
        for copy in first[c] + second[c] + (third[c],) + ring[c] + onward[c]:
            copy.wait_send()

        def drain(i, _, c=c):
            t = lax.rem(s + i, sections)
            own_copy(c, t).wait_send()
            far_copy(c, t).wait_send()
            mom_copy(c, t).wait_send()
            return 0

        lax.fori_loop(1, sections, drain, 0)
        far_copy(c, s).wait_send()


def body(gradients, master, moment_one, moment_two, new_owner):
    sections = lax.axis_size("section")
    blocks, rows, lanes = master.shape
    bf16 = jnp.bfloat16
    f32 = jnp.float32
    grads = gradients.reshape(blocks, 2, 4, rows, lanes)
    owners = new_owner.reshape(1, -1)
    vmem = pl.BlockSpec(memory_space=pltpu.VMEM)
    state_shape = jax.ShapeDtypeStruct((sections, PAIR, rows, lanes), f32)
    dma = pltpu.SemaphoreType.DMA
    out = pl.pallas_call(
        functools.partial(kernel, sections),
        out_shape=(
            state_shape,
            state_shape,
            state_shape,
            jax.ShapeDtypeStruct((sections, PAIR, 2, 4, rows, lanes), bf16),
        ),
        in_specs=[
            pl.BlockSpec(memory_space=pltpu.SMEM),
            pl.BlockSpec(memory_space=pl.ANY),
            vmem,
            vmem,
            vmem,
        ],
        out_specs=(vmem, vmem, vmem, vmem),
        scratch_shapes=[
            pltpu.VMEM((blocks, 2, rows, lanes), bf16),
            pltpu.VMEM((2, blocks, rows, lanes), bf16),
            pltpu.VMEM((2, blocks, rows, lanes), bf16),
            pltpu.VMEM((2, blocks, rows, lanes), bf16),
            pltpu.VMEM((2, 2, blocks, rows, lanes), bf16),
            pltpu.VMEM((blocks, rows, lanes), bf16),
            pltpu.VMEM((blocks, rows, lanes), bf16),
            pltpu.VMEM((3, blocks, rows, lanes), bf16),
            pltpu.VMEM((sections, 3, PAIR, rows, lanes), bf16),
            pltpu.VMEM((sections, 2, PAIR, rows, lanes), bf16),
            pltpu.SMEM((sections * PAIR,), jnp.int32),
            pltpu.SMEM((sections * PAIR,), jnp.int32),
            dma((PARTS, 3)),
            dma((PARTS, 4)),
            dma((PARTS, 4)),
            dma((PARTS, 2)),
            dma((PARTS, 2)),
            dma((PARTS,)),
            dma((PARTS,)),
            dma((PARTS, sections)),
            dma((PARTS, sections)),
            dma((PARTS, sections)),
            dma((PARTS, sections)),
            dma((PARTS, sections)),
            dma((PARTS, sections)),
            dma((PARTS, 4)),
            dma((PARTS, 4)),
            dma((PARTS, 2)),
            dma((PARTS, 2)),
        ],
        compiler_params=pltpu.CompilerParams(
            collective_id=0, has_side_effects=True, vmem_limit_bytes=40 << 20
        ),
    )(owners, grads, master, moment_one, moment_two)
    weights = out[3].reshape(1, sections, PAIR, 8 * rows, lanes)
    return (out[0][None], out[1][None], out[2][None], weights)


def solution(mesh):
    placed = (
        P("replica", "section", None, None),
        P("section", "replica", None),
        P("section", "replica", None),
        P("section", "replica", None),
        P(),
    )
    return jax.shard_map(
        body,
        mesh=mesh,
        in_specs=placed,
        out_specs=(
            P("section", None, None, "replica", None),
            P("section", None, None, "replica", None),
            P("section", None, None, "replica", None),
            P("section", None, None, None, None),
        ),
        check_vma=False,
    )
```

time: 253 us -> 92.7 us (0.37)
  blocking collectives: 125 us -> 0 us
  waiting for transfers between devices: 87.4 us -> 0 us
  Pallas kernels: 0 us -> 81 us
  between operations: 14.1 us -> 0.65 us
  other arithmetic: 9.64 us -> 0 us
  local copies, waits for them, and re-layouts: 16.1 us -> 10.3 us
    all_to_all x4 -> x0, blocking collectives: 125 us -> none  [the longest x1 55.9 us: body(): lax.all_to_all(packed_grads, 'section', split_axis=0, concat_axis=0, tile...]
    pallas_call x0 -> x1, Pallas kernels: none -> 81 us  [body(): pl.pallas_call(functools.partial(kernel, sections), out_shape=(state_shap...]
    all_gather x1 -> x0, waiting for transfers between devices: 71.1 us -> none  [body(): lax.all_gather(out_master.astype(jnp.bfloat16), 'replica', axis=2, tiled=...]
    reduce_scatter x1 -> x0, waiting for transfers between devices: 16.2 us -> none  [body(): lax.psum_scatter(arrived.astype(jnp.float32).astype(jnp.bfloat16), 'repli...]
    gather x4 -> x0, local copies, waits for them, and re-layouts: 10 us -> none  [pack(): gathered = jnp.take(values, chosen, axis=0)]
    unnamed x3 -> x14, local copies, waits for them, and re-layouts: 4.66 us -> 10.3 us
    select_n x4 -> x0, other arithmetic: 4.8 us -> none  [the longest x2 4.79 us: pack(): jnp.where(filled[:, None, None], gathered, jnp.zeros((), values.dtype))]
    convert_element_type x1 -> x0, other arithmetic: 4.38 us -> none  [body(): out_master.astype(jnp.bfloat16)]
  transfers between devices with their start and end apart: 2 -> 0, of which waited for: 2 -> 0; matrix products, arithmetic and copies ran while one was open for 4% -> 0% of each run, Pallas kernels for 0% -> 0%
where the time goes in v1:
time: 92.7 us; the launch traced here: 92 us
  Pallas kernels  81 us (87%)
  local copies, waits for them, and re-layouts  10.3 us (11%)
    pallas_call x1, Pallas kernels, body(): pl.pallas_call(functools.partial(kernel, sections), out_shape=(state_shap...  81 us
    unnamed x14, local copies, waits for them, and re-layouts  10.3 us

profile of v1, /device:TPU:1, one launch (start us, length us, event | category | flops | bytes accessed | tf_op | source)
XLA Modules:
  0.0 92.0 jit_solution(15913741767514108860)
XLA Ops:
  0.6 0.0 copy-start
  0.6 1.6 %copy-done = bf16[1,16,512,128]{3,2,1,0:T(8,128)(2,1)S(1)} copy-done((bf16[1,16,512,128]{3,2,1,0:T(8,128)(2,1)S(1)}, bf16[1,16,512,128]{3,2,1,0:T(8,128)(2,1)}, u32[]{:S(2)}) %copy-start) | copy-done | bytes 2097176
  2.2 0.0 copy-start.1
  2.2 1.0 %copy-done.1 = f32[16,64,128]{2,1,0:T(8,128)S(1)} copy-done((f32[16,64,128]{2,1,0:T(8,128)S(1)}, f32[16,64,128]{2,1,0:T(8,128)}, u32[]{:S(2)}) %copy-start.1) | copy-done | bytes 524312
  3.3 0.0 copy-start.2
  3.3 1.0 %copy-done.2 = f32[16,64,128]{2,1,0:T(8,128)S(1)} copy-done((f32[16,64,128]{2,1,0:T(8,128)S(1)}, f32[16,64,128]{2,1,0:T(8,128)}, u32[]{:S(2)}) %copy-start.2) | copy-done | bytes 524312
  4.3 0.0 copy-start.3
  4.3 1.0 %copy-done.3 = f32[16,64,128]{2,1,0:T(8,128)S(1)} copy-done((f32[16,64,128]{2,1,0:T(8,128)S(1)}, f32[16,64,128]{2,1,0:T(8,128)}, u32[]{:S(2)}) %copy-start.3) | copy-done | bytes 524312
  5.4 0.0 copy-start.4
  5.4 0.7 copy-done.4
  6.0 81.0 %shard_map.84 = (f32[16,2,64,128]{3,2,1,0:T(8,128)S(1)}, f32[16,2,64,128]{3,2,1,0:T(8,128)S(1)}, f32[16,2,64,128]{3,2,1,0:T(8,128)S(1)}, bf16[16,2,2,4,64,128]{5,4,3,2,1,0:T(8,128)(2,1)S(1)}) custom-call(s32[1,256]{1,0:T(1,128)S(1)} %bitcast.11, bf16[16,2,4,64,128]{4,3,2,1,0:T(8,128)(2,1)S(1)} %bitcast.7, f32[16,64,128]{2,1,0:T(8,128)S(1)} %copy-done.1, ...), custom_call_target="tpu_custom_call" | custom-call | tf_op jit(solution)/shard_map/pallas_call | solution.py:343
  87.1 1.0 %copy.13 = f32[1,16,2,64,128]{4,3,2,1,0:T(8,128)} copy(f32[1,16,2,64,128]{4,3,2,1,0:T(8,128)S(1)} %bitcast.10) | data formatting | bytes 2097152
  88.0 1.0 %copy.14 = f32[1,16,2,64,128]{4,3,2,1,0:T(8,128)} copy(f32[1,16,2,64,128]{4,3,2,1,0:T(8,128)S(1)} %bitcast.9) | data formatting | bytes 2097152
  89.0 1.0 %copy.15 = f32[1,16,2,64,128]{4,3,2,1,0:T(8,128)} copy(f32[1,16,2,64,128]{4,3,2,1,0:T(8,128)S(1)} %bitcast.8) | data formatting | bytes 2097152
  90.0 2.0 %copy.16 = bf16[1,16,2,512,128]{4,3,2,1,0:T(8,128)(2,1)} copy(bf16[1,16,2,512,128]{4,3,2,1,0:T(8,128)(2,1)S(1)} %bitcast.6) | data formatting | bytes 8388608
Async XLA Ops:
  0.6 1.6 %copy-start = (bf16[1,16,512,128]{3,2,1,0:T(8,128)(2,1)S(1)}, bf16[1,16,512,128]{3,2,1,0:T(8,128)(2,1)}, u32[]{:S(2)}) copy-start(bf16[1,16,512,128]{3,2,1,0:T(8,128)(2,1)} %param.5) | copy-start | bytes 6291460
  2.2 1.0 %copy-start.1 = (f32[16,64,128]{2,1,0:T(8,128)S(1)}, f32[16,64,128]{2,1,0:T(8,128)}, u32[]{:S(2)}) copy-start(f32[16,64,128]{2,1,0:T(8,128)} %master_ref.1) | copy-start | bytes 1572868
  3.3 1.0 %copy-start.2 = (f32[16,64,128]{2,1,0:T(8,128)S(1)}, f32[16,64,128]{2,1,0:T(8,128)}, u32[]{:S(2)}) copy-start(f32[16,64,128]{2,1,0:T(8,128)} %one_ref.1) | copy-start | bytes 1572868
  4.3 1.0 %copy-start.3 = (f32[16,64,128]{2,1,0:T(8,128)S(1)}, f32[16,64,128]{2,1,0:T(8,128)}, u32[]{:S(2)}) copy-start(f32[16,64,128]{2,1,0:T(8,128)} %two_ref.1) | copy-start | bytes 1572868
  5.4 0.7 copy-start.4

commit v2 on v1

v2 whole, which is shorter than its diff:
```python
import functools

import jax
import jax.numpy as jnp
from jax import lax
from jax.experimental import pallas as pl
from jax.experimental.pallas import tpu as pltpu
from jax.sharding import PartitionSpec as P

MESH = pl.DeviceIdType.MESH
PAIR = 2
PARTS = 4
X_FIRST = (False, False, False, False)

beta_one = 0.9
beta_two = 0.95
step_count = 10.0
learn_rate = 0.01
decay_rate = 0.1
epsilon = 1e-08
correct_one = 1.0 - beta_one**step_count
correct_two = 1.0 - beta_two**step_count


def adamw_update(master, moment_one, moment_two, gradient):
    upd_one = beta_one * moment_one + (1.0 - beta_one) * gradient
    upd_two = beta_two * moment_two + (1.0 - beta_two) * gradient * gradient
    direction = upd_one / correct_one / (jnp.sqrt(upd_two / correct_two) + epsilon)
    upd_master = master - learn_rate * (direction + decay_rate * master)
    return (upd_master, upd_one, upd_two)


def kernel(
    sections,
    owner_hbm,
    grads_ref,
    master_hbm,
    one_hbm,
    two_hbm,
    out_master,
    out_one,
    out_two,
    weights,
    owner_ref,
    state_ref,
    own,
    near,
    half_out,
    half_in,
    upd,
    sendbuf,
    moments,
    chosen,
    filled,
    owner_sem,
    state_sem,
    load_sem,
    met_row,
    met_far,
    first_send,
    first_recv,
    half_send,
    half_recv,
    mom_send,
    mom_recv,
    own_send,
    own_recv,
    far_send,
    far_recv,
    ring_send,
    ring_recv,
    fwd_send,
    fwd_recv,
):
    blocks, rows = upd.shape[1], upd.shape[2]
    part_rows = rows // PARTS
    f32, bf16 = jnp.float32, jnp.bfloat16
    r = lax.axis_index("replica")
    s = lax.axis_index("section")
    xh = r // 4
    z = r % 4
    up = lax.rem(z + 1, 4)
    down = lax.rem(z + 3, 4)
    opposite = lax.rem(z + 2, 4)
    around = (up, down, opposite)
    dev_up = (xh * 4 + up, s)
    dev_down = (xh * 4 + down, s)
    dev_around = (dev_up, dev_down, (xh * 4 + opposite, s))
    partner = (1 - xh) * 4 + z

    def part(c):
        return pl.ds(c * part_rows, part_rows)

    def remote(src, dst, send, recv, device):
        return pltpu.make_async_remote_copy(
            src_ref=src, dst_ref=dst, send_sem=send, recv_sem=recv,
            device_id=device, device_id_type=MESH,
        )

    barrier = pltpu.get_barrier_semaphore()
    quad = [(s // 4) * 4 + lax.rem(s + i, 4) for i in range(1, 4)]
    row = [lax.rem(s + 4 * i, 16) for i in range(1, 4)]
    for device in dev_around + ((partner, s),):
        pl.semaphore_signal(barrier, inc=1, device_id=device, device_id_type=MESH)
    for t in quad + row:
        pl.semaphore_signal(barrier, inc=1, device_id=(r, t), device_id_type=MESH)

    owner_load = pltpu.make_async_copy(owner_hbm, owner_ref, owner_sem)
    owner_load.start()
    loads = []
    for c in range(PARTS):
        src = grads_ref.at[:, xh, :, part(c)] if X_FIRST[c] else grads_ref.at[:, :, z, part(c)]
        dst = own.at[:, :, part(c)] if X_FIRST[c] else own.at[:, pl.ds(0, 2), part(c)]
        loads.append(pltpu.make_async_copy(src, dst, load_sem.at[c]))
        loads[c].start()
    state_loads = []
    for k, src in enumerate((master_hbm, one_hbm, two_hbm)):
        state_loads.append(pltpu.make_async_copy(src, state_ref.at[k], state_sem.at[k]))
        state_loads[k].start()

    pl.semaphore_wait(barrier, 10)
    for t in row:
        pl.semaphore_signal(met_row, inc=1, device_id=(r, t), device_id_type=MESH)

    first = []
    for c in range(PARTS):
        rc = part(c)
        if X_FIRST[c]:
            first.append((
                remote(grads_ref.at[:, 1 - xh, :, rc], near.at[:, pl.ds(0, 4), rc], first_send.at[c, 0], first_recv.at[c, 0], (partner, s)),
            ))
        else:
            first.append(tuple(
                remote(grads_ref.at[:, :, around[k], rc], near.at[:, pl.ds(2 * k, 2), rc], first_send.at[c, k], first_recv.at[c, k], dev_around[k])
                for k in (2, 0, 1)
            ))
        for copy in first[c]:
            copy.start()

    owner_load.wait()
    for t in range(sections):
        one_at = jnp.int32(0)
        last_at = jnp.int32(0)
        count = jnp.int32(0)
        for i in reversed(range(blocks)):
            same = owner_ref[0, s * blocks + i] == t
            one_at = jnp.where(same, i, one_at)
            last_at = jnp.where(same & (count == 0), i, last_at)
            count = count + jnp.where(same, 1, 0)
        chosen[t * PAIR] = one_at
        chosen[t * PAIR + 1] = last_at
        filled[t * PAIR] = jnp.where(count > 0, 1, 0)
        filled[t * PAIR + 1] = jnp.where(count > 1, 1, 0)

    pl.semaphore_wait(met_row, 3)
    pl.semaphore_signal(met_far, inc=1, device_id=(partner, s), device_id_type=MESH)

    def first_sum(c, b, h):
        rc = part(c)
        total = own[b, h, rc].astype(f32)
        if X_FIRST[c]:
            return total + near[b, h, rc].astype(f32)
        for k in range(3):
            total = total + near[b, 2 * k + h, rc].astype(f32)
        return total

    second = [None] * PARTS

    def cross(c):
        rc = part(c)
        loads[c].wait()
        for copy in first[c]:
            copy.wait_recv()
        targets = tuple(zip(around, dev_around)) if X_FIRST[c] else ((1 - xh, (partner, s)),)
        second[c] = tuple(
            remote(half_out.at[k, :, rc], half_in.at[k, :, rc], half_send.at[c, k], half_recv.at[c, k], device)
            for k, (_, device) in enumerate(targets)
        )
        for k, (h, _) in enumerate(targets):

            def add(b, _, k=k, h=h):
                half_out[k, b, rc] = first_sum(c, b, h).astype(bf16)
                return 0

            lax.fori_loop(0, blocks, add, 0)
            second[c][k].start()

    def mom_copy(c, t):
        return remote(
            sendbuf.at[t, pl.ds(1, 2), :, part(c)], moments.at[s, :, :, part(c)],
            mom_send.at[c, t], mom_recv.at[c, s], (r, t),
        )

    def own_copy(c, t):
        return remote(
            sendbuf.at[t, 0, :, part(c)], weights.at[s, :, xh, z, part(c)],
            own_send.at[c, t], own_recv.at[c, s], (r, t),
        )

    def far_copy(c, t):
        return remote(
            sendbuf.at[t, 0, :, part(c)], weights.at[s, :, xh, z, part(c)],
            far_send.at[c, t], far_recv.at[c, s], (partner, t),
        )

    def update(c):
        rc = part(c)
        if c == 0:
            for copy in state_loads:
                copy.wait()
            pl.semaphore_wait(met_far, 1)
        for copy in second[c]:
            copy.wait_recv()

        def step(b, _):
            gradient = first_sum(c, b, z if X_FIRST[c] else xh)
            for k in range(len(second[c])):
                gradient = gradient + half_in[k, b, rc].astype(f32)
            new = adamw_update(state_ref[0, b, rc], state_ref[1, b, rc], state_ref[2, b, rc], gradient)
            for k in range(3):
                upd[k, b, rc] = new[k].astype(bf16)
            return 0

        lax.fori_loop(0, blocks, step, 0)

        def pack(t):
            for j in range(PAIR):
                index = chosen[t * PAIR + j]
                there = filled[t * PAIR + j] != 0
                for k in range(3):
                    value = upd[k, index, rc]
                    sendbuf[t, k, j, rc] = jnp.where(there, value, jnp.zeros_like(value))

        def deliver(i, _):
            t = lax.rem(s + i, sections)
            pack(t)
            own_copy(c, t).start()
            far_copy(c, t).start()
            mom_copy(c, t).start()
            return 0

        lax.fori_loop(1, sections, deliver, 0)
        pack(s)
        far_copy(c, s).start()
        for j in range(PAIR):
            weights[s, j, xh, z, rc] = sendbuf[s, 0, j, rc]
            moments[s, 0, j, rc] = sendbuf[s, 1, j, rc]
            moments[s, 1, j, rc] = sendbuf[s, 2, j, rc]

    def arrived(ref_of, sem_of, device):
        return remote(ref_of, ref_of, sem_of, sem_of, device)

    ring = [None] * PARTS

    def gather(c):
        rc = part(c)

        def take(i, _):
            t = lax.rem(s + i, sections)
            arrived(weights.at[t, :, xh, z, rc], own_recv.at[c, t], (r, t)).wait_recv()
            arrived(weights.at[t, :, 1 - xh, z, rc], far_recv.at[c, t], (partner, t)).wait_recv()
            return 0

        lax.fori_loop(1, sections, take, 0)
        arrived(weights.at[s, :, 1 - xh, z, rc], far_recv.at[c, s], (partner, s)).wait_recv()

        def along(h, k, device):
            ref = weights.at[:, :, h, z, rc]
            return remote(ref, ref, ring_send.at[c, k], ring_recv.at[c, k], device)

        ring[c] = (along(0, 0, dev_up), along(1, 1, dev_down), along(1, 2, dev_up), along(0, 3, dev_down))
        for copy in ring[c]:
            copy.start()

    onward = [None] * PARTS

    def forward(c):
        rc = part(c)
        from_down = weights.at[:, :, 0, down, rc]
        from_up = weights.at[:, :, 1, up, rc]
        onward[c] = (
            remote(from_down, from_down, fwd_send.at[c, 0], fwd_recv.at[c, 0], dev_up),
            remote(from_up, from_up, fwd_send.at[c, 1], fwd_recv.at[c, 1], dev_down),
        )
        arrived(from_down, ring_recv.at[c, 0], dev_down).wait_recv()
        onward[c][0].start()
        arrived(from_up, ring_recv.at[c, 1], dev_up).wait_recv()
        onward[c][1].start()

    def state(c):
        rc = part(c)

        def take(i, _):
            t = lax.rem(s + i, sections)
            arrived(moments.at[t, :, :, rc], mom_recv.at[c, t], (r, t)).wait_recv()
            return 0

        lax.fori_loop(1, sections, take, 0)

        def widen(t, _):
            for j in range(PAIR):
                out_master[t, j, rc] = weights[t, j, xh, z, rc].astype(f32)
                out_one[t, j, rc] = moments[t, 0, j, rc].astype(f32)
                out_two[t, j, rc] = moments[t, 1, j, rc].astype(f32)
            return 0

        lax.fori_loop(0, sections, widen, 0)

    stages = (cross, update, gather, forward, state)
    for tick in range(PARTS + len(stages) - 1):
        for number in reversed(range(len(stages))):
            c = tick - number
            if 0 <= c < PARTS:
                stages[number](c)

    for c in range(PARTS):
        rc = part(c)
        arrived(weights.at[:, :, 1, down, rc], ring_recv.at[c, 2], dev_down).wait_recv()
        arrived(weights.at[:, :, 0, up, rc], ring_recv.at[c, 3], dev_up).wait_recv()
        arrived(weights.at[:, :, 0, opposite, rc], fwd_recv.at[c, 0], dev_down).wait_recv()
        arrived(weights.at[:, :, 1, opposite, rc], fwd_recv.at[c, 1], dev_up).wait_recv()
        for copy in first[c] + second[c] + ring[c] + onward[c]:
            copy.wait_send()

        def drain(i, _, c=c):
            t = lax.rem(s + i, sections)
            own_copy(c, t).wait_send()
            far_copy(c, t).wait_send()
            mom_copy(c, t).wait_send()
            return 0

        lax.fori_loop(1, sections, drain, 0)
        far_copy(c, s).wait_send()


def store(*refs):
    count = len(refs) // 2
    sems = refs[-1]
    copies = [pltpu.make_async_copy(refs[k], refs[count + k], sems.at[k]) for k in range(count)]
    for copy in copies:
        copy.start()
    for copy in copies:
        copy.wait()


def body(gradients, master, moment_one, moment_two, new_owner):
    sections = lax.axis_size("section")
    blocks, rows, lanes = master.shape
    bf16 = jnp.bfloat16
    f32 = jnp.float32
    grads = gradients.reshape(blocks, 2, 4, rows, lanes)
    owners = new_owner.reshape(1, -1)
    vmem = pl.BlockSpec(memory_space=pltpu.VMEM)
    hbm = pl.BlockSpec(memory_space=pltpu.HBM)
    state_shape = jax.ShapeDtypeStruct((sections, PAIR, rows, lanes), f32)
    weight_shape = jax.ShapeDtypeStruct((sections, PAIR, 2, 4, rows, lanes), bf16)
    dma = pltpu.SemaphoreType.DMA
    regular = pltpu.SemaphoreType.REGULAR
    out = pl.pallas_call(
        functools.partial(kernel, sections),
        out_shape=(state_shape, state_shape, state_shape, weight_shape),
        in_specs=[hbm] * 5,
        out_specs=(vmem, vmem, vmem, vmem),
        scratch_shapes=[
            pltpu.SMEM(owners.shape, jnp.int32),
            pltpu.VMEM((3, blocks, rows, lanes), f32),
            pltpu.VMEM((blocks, 4, rows, lanes), bf16),
            pltpu.VMEM((blocks, 6, rows, lanes), bf16),
            pltpu.VMEM((3, blocks, rows, lanes), bf16),
            pltpu.VMEM((3, blocks, rows, lanes), bf16),
            pltpu.VMEM((3, blocks, rows, lanes), bf16),
            pltpu.VMEM((sections, 3, PAIR, rows, lanes), bf16),
            pltpu.VMEM((sections, 2, PAIR, rows, lanes), bf16),
            pltpu.SMEM((sections * PAIR,), jnp.int32),
            pltpu.SMEM((sections * PAIR,), jnp.int32),
            dma(()),
            dma((3,)),
            dma((PARTS,)),
            regular,
            regular,
            dma((PARTS, 3)),
            dma((PARTS, 3)),
            dma((PARTS, 3)),
            dma((PARTS, 3)),
            dma((PARTS, sections)),
            dma((PARTS, sections)),
            dma((PARTS, sections)),
            dma((PARTS, sections)),
            dma((PARTS, sections)),
            dma((PARTS, sections)),
            dma((PARTS, 4)),
            dma((PARTS, 4)),
            dma((PARTS, 2)),
            dma((PARTS, 2)),
        ],
        compiler_params=pltpu.CompilerParams(
            collective_id=0, has_side_effects=True, vmem_limit_bytes=40 << 20
        ),
    )(*[pltpu.with_memory_space_constraint(a, pltpu.HBM) for a in (owners, grads, master, moment_one, moment_two)])
    out = pl.pallas_call(
        store,
        out_shape=(state_shape, state_shape, state_shape, weight_shape),
        in_specs=[pl.BlockSpec(memory_space=pl.ANY)] * 4,
        out_specs=(hbm,) * 4,
        scratch_shapes=[dma((4,))],
        compiler_params=pltpu.CompilerParams(vmem_limit_bytes=1 << 20),
    )(*out)
    weights = out[3].reshape(1, sections, PAIR, 8 * rows, lanes)
    return (out[0][None], out[1][None], out[2][None], weights)


def solution(mesh):
    placed = (
        P("replica", "section", None, None),
        P("section", "replica", None),
        P("section", "replica", None),
        P("section", "replica", None),
        P(),
    )
    return jax.shard_map(
        body,
        mesh=mesh,
        in_specs=placed,
        out_specs=(
            P("section", None, None, "replica", None),
            P("section", None, None, "replica", None),
            P("section", None, None, "replica", None),
            P("section", None, None, None, None),
        ),
        check_vma=False,
    )
```

time: 92.7 us -> 75.8 us (0.82)
  local copies, waits for them, and re-layouts: 10.3 us -> 0 us
  Pallas kernels: 81 us -> 75 us
    unnamed x14 -> x0, local copies, waits for them, and re-layouts: 10.3 us -> none
    pallas_call x1, Pallas kernels: 81 us -> 72 us  [body(): pl.pallas_call(functools.partial(kernel, sections), out_shape=(state_shap...]
    pallas_call x0 -> x1, Pallas kernels: none -> 3.09 us  [body(): pl.pallas_call(store, out_shape=(state_shape, state_shape, state_shape, w...]
where the time goes in v2:
time: 75.8 us; the launch traced here: 75.7 us
  Pallas kernels  75 us (99%)
    pallas_call x1, Pallas kernels, body(): pl.pallas_call(functools.partial(kernel, sections), out_shape=(state_shap...  72 us
    pallas_call x1, Pallas kernels, body(): pl.pallas_call(store, out_shape=(state_shape, state_shape, state_shape, w...  3.09 us

profile of v2, /device:TPU:1, one launch (start us, length us, event | category | flops | bytes accessed | tf_op | source)
XLA Modules:
  0.0 75.7 jit_solution(15730954550645648928)
XLA Ops:
  0.6 72.0 %shard_map.84 = (f32[16,2,64,128]{3,2,1,0:T(8,128)S(1)}, f32[16,2,64,128]{3,2,1,0:T(8,128)S(1)}, f32[16,2,64,128]{3,2,1,0:T(8,128)S(1)}, bf16[16,2,2,4,64,128]{5,4,3,2,1,0:T(8,128)(2,1)S(1)}) custom-call(s32[1,256]{1,0:T(1,128)} %bitcast.7, bf16[16,2,4,64,128]{4,3,2,1,0:T(8,128)(2,1)} %bitcast.6, f32[16,64,128]{2,1,0:T(8,128)} %master_hbm.1, ...), custom_call_target="tpu_custom_call" | custom-call | tf_op jit(solution)/shard_map/pallas_call | solution.py:359
  72.6 3.1 %shard_map.85 = (f32[16,2,64,128]{3,2,1,0:T(8,128)}, f32[16,2,64,128]{3,2,1,0:T(8,128)}, f32[16,2,64,128]{3,2,1,0:T(8,128)}, bf16[16,2,2,4,64,128]{5,4,3,2,1,0:T(8,128)(2,1)}) custom-call(f32[16,2,64,128]{3,2,1,0:T(8,128)S(1)} %get-tuple-element.12.refs_0_, f32[16,2,64,128]{3,2,1,0:T(8,128)S(1)} %get-tuple-element.13.refs_1_, ...), custom_call_target="tpu_custom_call" | custom-call | tf_op jit(solution)/shard_map/pallas_call | solution.py:400

commit v3 on v2

--- a/solution.py
+++ b/solution.py
@@ -10,7 +10,10 @@
 MESH = pl.DeviceIdType.MESH
 PAIR = 2
 PARTS = 4
-X_FIRST = (False, False, False, False)
+DIRECT, JOIN, X_FIRST = range(3)
+SUMS = (JOIN, JOIN, X_FIRST, JOIN)
+Z_FIRST = (False, True, False, False)
+ORDER = "j0 j1 x0 j2 x1 u0 j3 x2 u1 g0 x3 u2 g1 f0 u3 g2 f1 s0 g3 f2 l1 s1 f3 s2 s3"
 
 beta_one = 0.9
 beta_two = 0.95
@@ -45,6 +48,8 @@
     state_ref,
     own,
     near,
+    mid_own,
+    mid_out,
     half_out,
     half_in,
     upd,
@@ -55,6 +60,9 @@
     owner_sem,
     state_sem,
     load_sem,
+    mid_sem,
+    mid_send,
+    mid_recv,
     met_row,
     met_far,
     first_send,
@@ -71,6 +79,8 @@
     ring_recv,
     fwd_send,
     fwd_recv,
+    pass_send,
+    pass_recv,
 ):
     blocks, rows = upd.shape[1], upd.shape[2]
     part_rows = rows // PARTS
@@ -109,10 +119,20 @@
     owner_load.start()
     loads = []
     for c in range(PARTS):
-        src = grads_ref.at[:, xh, :, part(c)] if X_FIRST[c] else grads_ref.at[:, :, z, part(c)]
-        dst = own.at[:, :, part(c)] if X_FIRST[c] else own.at[:, pl.ds(0, 2), part(c)]
+        by_x = SUMS[c] == X_FIRST
+        src = grads_ref.at[:, xh, :, part(c)] if by_x else grads_ref.at[:, :, z, part(c)]
+        dst = own.at[:, :, part(c)] if by_x else own.at[:, pl.ds(0, 2), part(c)]
         loads.append(pltpu.make_async_copy(src, dst, load_sem.at[c]))
         loads[c].start()
+    mid_loads = {}
+    for c in range(PARTS):
+        if SUMS[c] == JOIN:
+            mid_loads[c] = (
+                pltpu.make_async_copy(grads_ref.at[:, 0, up, part(c)], mid_own.at[0, :, part(c)], mid_sem.at[c, 0]),
+                pltpu.make_async_copy(grads_ref.at[:, 1, down, part(c)], mid_own.at[1, :, part(c)], mid_sem.at[c, 1]),
+            )
+            for copy in mid_loads[c]:
+                copy.start()
     state_loads = []
     for k, src in enumerate((master_hbm, one_hbm, two_hbm)):
         state_loads.append(pltpu.make_async_copy(src, state_ref.at[k], state_sem.at[k]))
@@ -125,9 +145,14 @@
     first = []
     for c in range(PARTS):
         rc = part(c)
-        if X_FIRST[c]:
+        if SUMS[c] == X_FIRST:
             first.append((
                 remote(grads_ref.at[:, 1 - xh, :, rc], near.at[:, pl.ds(0, 4), rc], first_send.at[c, 0], first_recv.at[c, 0], (partner, s)),
+            ))
+        elif SUMS[c] == JOIN:
+            first.append(tuple(
+                remote(grads_ref.at[:, h, around[of], rc], near.at[:, slot, rc], first_send.at[c, k], first_recv.at[c, k], dev_around[to])
+                for k, (h, of, to, slot) in enumerate(((0, 2, 0, 4), (1, 2, 1, 5), (1, 0, 0, 1), (0, 1, 1, 2)))
             ))
         else:
             first.append(tuple(
@@ -158,20 +183,41 @@
     def first_sum(c, b, h):
         rc = part(c)
         total = own[b, h, rc].astype(f32)
-        if X_FIRST[c]:
+        if SUMS[c] == X_FIRST:
             return total + near[b, h, rc].astype(f32)
-        for k in range(3):
+        for k in range(2 if SUMS[c] == JOIN else 3):
             total = total + near[b, 2 * k + h, rc].astype(f32)
         return total
 
+    joined = [()] * PARTS
+
+    def join(c):
+        if SUMS[c] != JOIN:
+            return
+        rc = part(c)
+        joined[c] = tuple(
+            remote(mid_out.at[h, :, rc], near.at[:, 3 * h, rc], mid_send.at[c, h], mid_recv.at[c, h], dev_around[h])
+            for h in range(2)
+        )
+        for h in range(2):
+            mid_loads[c][h].wait()
+            first[c][h].wait_recv()
+
+            def add(b, _, h=h):
+                mid_out[h, b, rc] = (near[b, 4 + h, rc].astype(f32) + mid_own[h, b, rc].astype(f32)).astype(bf16)
+                return 0
+
+            lax.fori_loop(0, blocks, add, 0)
+            joined[c][h].start()
+
     second = [None] * PARTS
 
     def cross(c):
         rc = part(c)
         loads[c].wait()
-        for copy in first[c]:
+        for copy in (first[c][2:] + joined[c]) if SUMS[c] == JOIN else first[c]:
             copy.wait_recv()
-        targets = tuple(zip(around, dev_around)) if X_FIRST[c] else ((1 - xh, (partner, s)),)
+        targets = tuple(zip(around, dev_around)) if SUMS[c] == X_FIRST else ((1 - xh, (partner, s)),)
         second[c] = tuple(
             remote(half_out.at[k, :, rc], half_in.at[k, :, rc], half_send.at[c, k], half_recv.at[c, k], device)
             for k, (_, device) in enumerate(targets)
@@ -213,7 +259,7 @@
             copy.wait_recv()
 
         def step(b, _):
-            gradient = first_sum(c, b, z if X_FIRST[c] else xh)
+            gradient = first_sum(c, b, z if SUMS[c] == X_FIRST else xh)
             for k in range(len(second[c])):
                 gradient = gradient + half_in[k, b, rc].astype(f32)
             new = adamw_update(state_ref[0, b, rc], state_ref[1, b, rc], state_ref[2, b, rc], gradient)
@@ -235,13 +281,15 @@
             t = lax.rem(s + i, sections)
             pack(t)
             own_copy(c, t).start()
-            far_copy(c, t).start()
+            if not Z_FIRST[c]:
+                far_copy(c, t).start()
             mom_copy(c, t).start()
             return 0
 
         lax.fori_loop(1, sections, deliver, 0)
         pack(s)
-        far_copy(c, s).start()
+        if not Z_FIRST[c]:
+            far_copy(c, s).start()
         for j in range(PAIR):
             weights[s, j, xh, z, rc] = sendbuf[s, 0, j, rc]
             moments[s, 0, j, rc] = sendbuf[s, 1, j, rc]
@@ -251,6 +299,13 @@
         return remote(ref_of, ref_of, sem_of, sem_of, device)
 
     ring = [None] * PARTS
+    onward = [None] * PARTS
+    passed = [()] * PARTS
+
+    def shard(c, half, at):
+        if Z_FIRST[c]:
+            return weights.at[:, half, xh, at, part(c)]
+        return weights.at[:, :, half, at, part(c)]
 
     def gather(c):
         rc = part(c)
@@ -258,26 +313,32 @@
         def take(i, _):
             t = lax.rem(s + i, sections)
             arrived(weights.at[t, :, xh, z, rc], own_recv.at[c, t], (r, t)).wait_recv()
-            arrived(weights.at[t, :, 1 - xh, z, rc], far_recv.at[c, t], (partner, t)).wait_recv()
+            if not Z_FIRST[c]:
+                arrived(weights.at[t, :, 1 - xh, z, rc], far_recv.at[c, t], (partner, t)).wait_recv()
             return 0
 
         lax.fori_loop(1, sections, take, 0)
-        arrived(weights.at[s, :, 1 - xh, z, rc], far_recv.at[c, s], (partner, s)).wait_recv()
-
-        def along(h, k, device):
-            ref = weights.at[:, :, h, z, rc]
+        if not Z_FIRST[c]:
+            arrived(weights.at[s, :, 1 - xh, z, rc], far_recv.at[c, s], (partner, s)).wait_recv()
+
+        def along(half, k, device):
+            ref = shard(c, half, z)
             return remote(ref, ref, ring_send.at[c, k], ring_recv.at[c, k], device)
 
         ring[c] = (along(0, 0, dev_up), along(1, 1, dev_down), along(1, 2, dev_up), along(0, 3, dev_down))
         for copy in ring[c]:
             copy.start()
-
-    onward = [None] * PARTS
+        if Z_FIRST[c]:
+            hand(c, weights.at[:, :, xh, z, rc], 0)
+
+    def hand(c, ref, k):
+        copy = remote(ref, ref, pass_send.at[c, k], pass_recv.at[c, k], (partner, s))
+        copy.start()
+        passed[c] += (copy,)
 
     def forward(c):
-        rc = part(c)
-        from_down = weights.at[:, :, 0, down, rc]
-        from_up = weights.at[:, :, 1, up, rc]
+        from_down = shard(c, 0, down)
+        from_up = shard(c, 1, up)
         onward[c] = (
             remote(from_down, from_down, fwd_send.at[c, 0], fwd_recv.at[c, 0], dev_up),
             remote(from_up, from_up, fwd_send.at[c, 1], fwd_recv.at[c, 1], dev_down),
@@ -286,6 +347,19 @@
         onward[c][0].start()
         arrived(from_up, ring_recv.at[c, 1], dev_up).wait_recv()
         onward[c][1].start()
+        if Z_FIRST[c]:
+            rc = part(c)
+            arrived(shard(c, 1, down), ring_recv.at[c, 2], dev_down).wait_recv()
+            hand(c, weights.at[:, :, xh, down, rc], 1)
+            arrived(shard(c, 0, up), ring_recv.at[c, 3], dev_up).wait_recv()
+            hand(c, weights.at[:, :, xh, up, rc], 2)
+
+    def last(c):
+        rc = part(c)
+        arrived(shard(c, 0, opposite), fwd_recv.at[c, 0], dev_down).wait_recv()
+        arrived(shard(c, 1, opposite), fwd_recv.at[c, 1], dev_up).wait_recv()
+        if Z_FIRST[c]:
+            hand(c, weights.at[:, :, xh, opposite, rc], 3)
 
     def state(c):
         rc = part(c)
@@ -306,31 +380,32 @@
 
         lax.fori_loop(0, sections, widen, 0)
 
-    stages = (cross, update, gather, forward, state)
-    for tick in range(PARTS + len(stages) - 1):
-        for number in reversed(range(len(stages))):
-            c = tick - number
-            if 0 <= c < PARTS:
-                stages[number](c)
+    stages = dict(j=join, x=cross, u=update, g=gather, f=forward, l=last, s=state)
+    for step in ORDER.split():
+        stages[step[0]](int(step[1]))
 
     for c in range(PARTS):
-        rc = part(c)
-        arrived(weights.at[:, :, 1, down, rc], ring_recv.at[c, 2], dev_down).wait_recv()
-        arrived(weights.at[:, :, 0, up, rc], ring_recv.at[c, 3], dev_up).wait_recv()
-        arrived(weights.at[:, :, 0, opposite, rc], fwd_recv.at[c, 0], dev_down).wait_recv()
-        arrived(weights.at[:, :, 1, opposite, rc], fwd_recv.at[c, 1], dev_up).wait_recv()
-        for copy in first[c] + second[c] + ring[c] + onward[c]:
+        if not Z_FIRST[c]:
+            last(c)
+            arrived(shard(c, 1, down), ring_recv.at[c, 2], dev_down).wait_recv()
+            arrived(shard(c, 0, up), ring_recv.at[c, 3], dev_up).wait_recv()
+        else:
+            for k, at in enumerate((z, down, up, opposite)):
+                arrived(weights.at[:, :, 1 - xh, at, part(c)], pass_recv.at[c, k], (partner, s)).wait_recv()
+        for copy in first[c] + joined[c] + second[c] + ring[c] + onward[c] + passed[c]:
             copy.wait_send()
 
         def drain(i, _, c=c):
             t = lax.rem(s + i, sections)
             own_copy(c, t).wait_send()
-            far_copy(c, t).wait_send()
+            if not Z_FIRST[c]:
+                far_copy(c, t).wait_send()
             mom_copy(c, t).wait_send()
             return 0
 
         lax.fori_loop(1, sections, drain, 0)
-        far_copy(c, s).wait_send()
+        if not Z_FIRST[c]:
+            far_copy(c, s).wait_send()
 
 
 def store(*refs):
@@ -366,6 +441,8 @@
             pltpu.VMEM((3, blocks, rows, lanes), f32),
             pltpu.VMEM((blocks, 4, rows, lanes), bf16),
             pltpu.VMEM((blocks, 6, rows, lanes), bf16),
+            pltpu.VMEM((2, blocks, rows, lanes), bf16),
+            pltpu.VMEM((2, blocks, rows, lanes), bf16),
             pltpu.VMEM((3, blocks, rows, lanes), bf16),
             pltpu.VMEM((3, blocks, rows, lanes), bf16),
             pltpu.VMEM((3, blocks, rows, lanes), bf16),
@@ -376,10 +453,13 @@
             dma(()),
             dma((3,)),
             dma((PARTS,)),
+            dma((PARTS, 2)),
+            dma((PARTS, 2)),
+            dma((PARTS, 2)),
             regular,
             regular,
-            dma((PARTS, 3)),
-            dma((PARTS, 3)),
+            dma((PARTS, 4)),
+            dma((PARTS, 4)),
             dma((PARTS, 3)),
             dma((PARTS, 3)),
             dma((PARTS, sections)),
@@ -392,6 +472,8 @@
             dma((PARTS, 4)),
             dma((PARTS, 2)),
             dma((PARTS, 2)),
+            dma((PARTS, 4)),
+            dma((PARTS, 4)),
         ],
         compiler_params=pltpu.CompilerParams(
             collective_id=0, has_side_effects=True, vmem_limit_bytes=40 << 20

time: 75.8 us -> 73 us (0.963)
  Pallas kernels: 75 us -> 71.5 us
    pallas_call x1, Pallas kernels: 72 us -> 68.4 us  [body(): pl.pallas_call(functools.partial(kernel, sections), out_shape=(state_shap...]
where the time goes in v3:
time: 73 us; the launch traced here: 72.1 us
  Pallas kernels  71.5 us (98%)
    pallas_call x1, Pallas kernels, body(): pl.pallas_call(functools.partial(kernel, sections), out_shape=(state_shap...  68.4 us
    pallas_call x1, Pallas kernels, body(): pl.pallas_call(store, out_shape=(state_shape, state_shape, state_shape, w...  3.09 us

profile of v3, /device:TPU:1, one launch (start us, length us, event | category | flops | bytes accessed | tf_op | source)
XLA Modules:
  0.0 72.1 jit_solution(15340885605761093360)
XLA Ops:
  0.6 68.4 %shard_map.84 = (f32[16,2,64,128]{3,2,1,0:T(8,128)S(1)}, f32[16,2,64,128]{3,2,1,0:T(8,128)S(1)}, f32[16,2,64,128]{3,2,1,0:T(8,128)S(1)}, bf16[16,2,2,4,64,128]{5,4,3,2,1,0:T(8,128)(2,1)S(1)}) custom-call(s32[1,256]{1,0:T(1,128)} %bitcast.7, bf16[16,2,4,64,128]{4,3,2,1,0:T(8,128)(2,1)} %bitcast.6, f32[16,64,128]{2,1,0:T(8,128)} %master_hbm.1, ...), custom_call_target="tpu_custom_call" | custom-call | tf_op jit(solution)/shard_map/pallas_call | solution.py:434
  69.1 3.1 %shard_map.85 = (f32[16,2,64,128]{3,2,1,0:T(8,128)}, f32[16,2,64,128]{3,2,1,0:T(8,128)}, f32[16,2,64,128]{3,2,1,0:T(8,128)}, bf16[16,2,2,4,64,128]{5,4,3,2,1,0:T(8,128)(2,1)}) custom-call(f32[16,2,64,128]{3,2,1,0:T(8,128)S(1)} %get-tuple-element.12.refs_0_, f32[16,2,64,128]{3,2,1,0:T(8,128)S(1)} %get-tuple-element.13.refs_1_, ...), custom_call_target="tpu_custom_call" | custom-call | tf_op jit(solution)/shard_map/pallas_call | solution.py:482

commit v4 on v3

--- a/solution.py
+++ b/solution.py
@@ -13,7 +13,13 @@
 DIRECT, JOIN, X_FIRST = range(3)
 SUMS = (JOIN, JOIN, X_FIRST, JOIN)
 Z_FIRST = (False, True, False, False)
-ORDER = "j0 j1 x0 j2 x1 u0 j3 x2 u1 g0 x3 u2 g1 f0 u3 g2 f1 s0 g3 f2 l1 s1 f3 s2 s3"
+ORDER = (
+    ("j", 0), ("j", 1), ("x", 0), ("j", 2), ("x", 1), ("u", 0),
+    ("j", 3), ("x", 2), ("u", 1), ("g", 0), ("x", 3), ("u", 2),
+    ("g", 1), ("f", 0), ("u", 3), ("g", 2), ("f", 1), ("g", 3),
+    ("f", 2), ("l", 1), ("f", 3), ("s", 0), ("s", 1), ("s", 2),
+    ("s", 3),
+)
 
 beta_one = 0.9
 beta_two = 0.95
@@ -381,8 +387,8 @@
         lax.fori_loop(0, sections, widen, 0)
 
     stages = dict(j=join, x=cross, u=update, g=gather, f=forward, l=last, s=state)
-    for step in ORDER.split():
-        stages[step[0]](int(step[1]))
+    for name, c in ORDER:
+        stages[name](c)
 
     for c in range(PARTS):
         if not Z_FIRST[c]:

time: 73 us -> 73 us (level)
  no operation moved by 1% of the time
where the time goes in v4:
time: 73 us; the launch traced here: 72.1 us
  Pallas kernels  71.5 us (98%)
    pallas_call x1, Pallas kernels, body(): pl.pallas_call(functools.partial(kernel, sections), out_shape=(state_shap...  68.4 us
    pallas_call x1, Pallas kernels, body(): pl.pallas_call(store, out_shape=(state_shape, state_shape, state_shape, w...  3.09 us

profile of v4, /device:TPU:1, one launch (start us, length us, event | category | flops | bytes accessed | tf_op | source)
XLA Modules:
  0.0 72.1 jit_solution(2851594264085317470)
XLA Ops:
  0.6 68.4 %shard_map.84 = (f32[16,2,64,128]{3,2,1,0:T(8,128)S(1)}, f32[16,2,64,128]{3,2,1,0:T(8,128)S(1)}, f32[16,2,64,128]{3,2,1,0:T(8,128)S(1)}, bf16[16,2,2,4,64,128]{5,4,3,2,1,0:T(8,128)(2,1)S(1)}) custom-call(s32[1,256]{1,0:T(1,128)} %bitcast.7, bf16[16,2,4,64,128]{4,3,2,1,0:T(8,128)(2,1)} %bitcast.6, f32[16,64,128]{2,1,0:T(8,128)} %master_hbm.1, ...), custom_call_target="tpu_custom_call" | custom-call | tf_op jit(solution)/shard_map/pallas_call | solution.py:440
  69.1 3.1 %shard_map.85 = (f32[16,2,64,128]{3,2,1,0:T(8,128)}, f32[16,2,64,128]{3,2,1,0:T(8,128)}, f32[16,2,64,128]{3,2,1,0:T(8,128)}, bf16[16,2,2,4,64,128]{5,4,3,2,1,0:T(8,128)(2,1)}) custom-call(f32[16,2,64,128]{3,2,1,0:T(8,128)S(1)} %get-tuple-element.12.refs_0_, f32[16,2,64,128]{3,2,1,0:T(8,128)S(1)} %get-tuple-element.13.refs_1_, ...), custom_call_target="tpu_custom_call" | custom-call | tf_op jit(solution)/shard_map/pallas_call | solution.py:488
